TPU v7x, 32 devices: a whole 2x2x4 slice. The times are simulated.
32 devices in a mesh: ctx: 4 (over y, x), tp: 2 (over core), dp: 4 (over z).
Axes of the slice: x: 2, y: 2, z: 4, core: 2. Of those that a mesh axis runs over, the one named last changes fastest.
Arguments:
- nucleotides: int32 [8192], P(('dp', 'ctx')), parts along dimension 0, may hold values from 0 to 3
- complement: int32 [4], replicated, may hold values from 0 to 3, each once
- embedding: float32 [4, 1024], replicated, may hold values from -6 to 6
- w_gate: float32 [1024, 2048], P(None, 'tp'), may hold values from -0.1875 to 0.1875
- w_value: float32 [1024, 2048], P(None, 'tp'), may hold values from -0.1875 to 0.1875
- w_state: float32 [1024, 256], replicated, may hold values from -0.1875 to 0.1875
- w_step: float32 [1024, 32], P(None, 'tp'), may hold values from -0.1875 to 0.1875
- step_bias: float32 [32], P('tp'), may hold values from -5.5 to -4.5
- decay_rate: float32 [32], P('tp'), may hold values from 0 to 3
- conv_value: float32 [4, 2048], P(None, 'tp'), may hold values from -3 to 3
- conv_state: float32 [4, 256], replicated, may hold values from -3 to 3
- skip_gain: float32 [32], P('tp'), may hold values from 0.5 to 2
- norm_weight: float32 [2048], P('tp'), may hold values from 0.1 to 1.9
- w_out: float32 [2048, 1024], P('tp'), may hold values from -0.125 to 0.125
Outputs:
- mixed: float32 [8192, 1024], P(('dp', 'ctx', 'tp')), parts along dimension 0
There are 4 independent parts, one for each index of `dp`. A program takes and returns all parts, laid end to end along the dimension named above; an argument that names none is the same for every part. Nothing has to cross between parts.
Inputs may be any that keep to these rules, and one draw needn't show every extreme that they name: `complement`: a permutation of the 4 nucleotide ids.
All inputs are finite; a program needn't handle non-finite values.
Results may differ from a plain program's by a relative error of at most 0.00023.
Values sent between devices are 32-bit elements; how exact they have to be, the bound alone decides.
A program may use at most 128 MiB of HBM per device.

v0:
```python
import functools

import jax
import jax.numpy as jnp
from jax import lax
from jax.experimental import pallas as pl
from jax.experimental.pallas import tpu as pltpu
from jax.sharding import PartitionSpec as P

EPSILON = 1e-05
LOG2E = 1.4426950408889634
F32 = jnp.float32
BF = jnp.bfloat16
MESH = pl.DeviceIdType.MESH
NT = (((1,), (1,)), ((), ()))
TN = (((0,), (0,)), ((), ()))
NN = (((1,), (0,)), ((), ()))


def dot(a, b, dims=NN):
    return lax.dot_general(a, b, dims, preferred_element_type=F32)


def split2(x):
    hi = x.astype(BF)
    return hi, (x - hi.astype(F32)).astype(BF)


def split3(x):
    hi = x.astype(BF)
    rest = x - hi.astype(F32)
    mid = rest.astype(BF)
    return hi, mid, (rest - mid.astype(F32)).astype(BF)


def dot3(a, b, dims=NN):
    ah, al = split2(a)
    bh, bl = split2(b)
    return dot(ah, bh, dims) + dot(al, bh, dims) + dot(ah, bl, dims)


def silu(x):
    return x / (1.0 + jnp.exp(-x))


def rows_of(x, count):
    return jnp.broadcast_to(x, (count, x.shape[1]))


def kernel(
    n, ids_ref, comp_ref, emb_ref, wg_ref, wv_ref, ws_ref, wstep_ref, bias_ref, decay_ref,
    cv_ref, cs_ref, skip_ref, nw_ref, wo_ref, out_ref,
    ids_all, tab, wout, wbuf, wsbuf, ebc, sproj, taps_f, taps_r, cnt_all, oh_all,
    vtab, xs, xp, gate, gated, lrow, lsrc, went, skb, gmat, cmat, btab, accs,
    loc_sem, id_send, id_recv, tab_send, tab_recv, wo_send, wo_recv, wo_loc,
):
    me = lax.axis_index("ctx")
    tp = lax.axis_index("tp")
    other = 1 - tp
    block = ids_ref.shape[1]
    half = wg_ref.shape[1]
    depth = wg_ref.shape[0]
    rows = block // 2
    heads_half = bias_ref.shape[1]
    heads = 2 * heads_half
    state = ws_ref.shape[1] // 2
    inner = 2 * half
    total = n * block
    pairs = inner // 128
    chunk = half // 2

    loads = []
    for i in range(4):
        src = (wv_ref, wg_ref)[i // 2]
        loads.append(
            pltpu.make_async_copy(
                src.at[:, pl.ds((i % 2) * chunk, chunk)], wbuf.at[i], loc_sem.at[i]
            )
        )
    loads.append(pltpu.make_async_copy(ws_ref, wsbuf, loc_sem.at[4]))
    for load in loads:
        load.start()
    wo_copy = pltpu.make_async_copy(wo_ref, wout.at[tp], wo_loc)

    barrier = pltpu.get_barrier_semaphore()
    for d in range(1, n):
        pl.semaphore_signal(
            barrier, inc=1, device_id={"ctx": lax.rem(me + d, n)}, device_id_type=MESH
        )
    pl.semaphore_signal(barrier, inc=1, device_id={"tp": other}, device_id_type=MESH)
    ids_all[me] = ids_ref[...]
    pl.semaphore_wait(barrier, n)
    id_copies = []
    for d in range(1, n):
        copy = pltpu.make_async_remote_copy(
            src_ref=ids_ref, dst_ref=ids_all.at[me],
            send_sem=id_send.at[d - 1], recv_sem=id_recv.at[d - 1],
            device_id={"ctx": lax.rem(me + d, n)}, device_id_type=MESH,
        )
        copy.start()
        id_copies.append(copy)
    wo_remote = pltpu.make_async_remote_copy(
        src_ref=wo_ref, dst_ref=wout.at[tp], send_sem=wo_send, recv_sem=wo_recv,
        device_id={"tp": other}, device_id_type=MESH,
    )
    wo_remote.start()

    emb = jnp.concatenate([emb_ref[...], jnp.zeros((4, depth), F32)], axis=0)
    emb_t = jnp.transpose(jnp.concatenate([emb] * 16, axis=0))
    for v in range(4):
        ebc[v] = jnp.broadcast_to(emb_t[:, v : v + 1], (depth, 128))

    def project(ref, width):
        def body(i, accs_in):
            at = pl.ds(pl.multiple_of(i * 8, 8), 8)
            w = ref[at, :]
            new = []
            for v in range(4):
                e = ebc[v, at, :]
                e = jnp.concatenate([e] * (width // 128), axis=1) if width > 128 else e[:, :width]
                new.append(accs_in[v] + e * w)
            return tuple(new)

        start = tuple(jnp.zeros((8, width), F32) for _ in range(4))
        done = lax.fori_loop(0, depth // 8, body, start, unroll=8)
        return [jnp.sum(a, axis=0, keepdims=True) for a in done]

    for i in range(4):
        loads[i].wait()
        parts = project(wbuf.at[i], chunk)
        base = 8 if i < 2 else 0
        for v in range(4):
            tab[tp, pl.ds(base + v, 1), pl.ds((i % 2) * chunk, chunk)] = parts[v]
    tab[tp, 16:20, :] = cv_ref[...]
    tab[tp, 24:25, :] = nw_ref[...]
    raw = project(wstep_ref, heads_half)
    for v in range(4):
        z = raw[v] + bias_ref[...]
        step = jnp.maximum(z, 0.0) + jnp.log1p(jnp.exp(-jnp.abs(z)))
        tab[tp, 32 + v : 33 + v, 0:heads_half] = step
    tab[tp, 36:37, 0:heads_half] = decay_ref[...]
    tab[tp, 37:38, 0:heads_half] = skip_ref[...]
    tab_copy = pltpu.make_async_remote_copy(
        src_ref=tab.at[tp], dst_ref=tab.at[tp], send_sem=tab_send, recv_sem=tab_recv,
        device_id={"tp": other}, device_id_type=MESH,
    )
    tab_copy.start()
    loads[4].wait()
    parts = project(wsbuf, 2 * state)
    for v in range(4):
        sproj[v : v + 1, :] = parts[v]
    wo_copy.start()

    for copy in id_copies:
        copy.wait()
    null = 4
    lane = lax.broadcasted_iota(jnp.int32, (8, block), 1)
    sub = lax.broadcasted_iota(jnp.int32, (8, block), 0)
    tri = (
        lax.broadcasted_iota(jnp.int32, (block, block), 0)
        <= lax.broadcasted_iota(jnp.int32, (block, block), 1)
    ).astype(BF)
    comp = [comp_ref[v] for v in range(4)]
    first_row = me * block + tp * rows
    running = jnp.zeros((8, 1), F32)
    before = jnp.zeros((8, 1), F32)
    through = jnp.zeros((8, 1), F32)
    for j in range(n):
        own = ids_all[j]
        blank = jnp.full((1, 128), null, jnp.int32)
        left = ids_all[j - 1][:, block - 128 :] if j > 0 else blank
        right = ids_all[j + 1][:, :128] if j < n - 1 else blank
        ext = rows_of(jnp.concatenate([left, own, right], axis=1), 8)
        cext = jnp.full_like(ext, null)
        for v in range(4):
            cext = jnp.where(ext == v, comp[v], cext)
        width = block + 256
        fwd = [pltpu.roll(ext, 3 - k, 1)[:, 128 : 128 + block] if k < 3 else ext[:, 128 : 128 + block] for k in range(4)]
        rev = [
            pltpu.roll(cext, width - (3 - k), 1)[:, 128 : 128 + block] if k < 3 else cext[:, 128 : 128 + block]
            for k in range(4)
        ]
        def pack(taps):
            return jnp.where(sub == 0, taps[0], jnp.where(sub == 1, taps[1], jnp.where(sub == 2, taps[2], taps[3])))
        def code(taps):
            return 64 * taps[0] + 16 * taps[1] + 4 * taps[2] + taps[3]
        code_f, code_r = code(fwd), code(rev)
        if j == 0:
            code_f = jnp.where(lane < 3, 256 + lane, code_f)
        if j == n - 1:
            code_r = jnp.where(lane >= block - 3, 264 - block + lane, code_r)
        taps_f[j] = jnp.where(sub == 4, code_f, pack(fwd))
        taps_r[j] = jnp.where(sub == 4, code_r, pack(rev))
        oh = (fwd[3] == sub).astype(F32)
        counts = dot(oh.astype(BF), tri) + running
        cnt_all[j] = counts
        oh_all[j] = oh
        running = running + jnp.sum(oh, axis=1, keepdims=True)
        t = lane + j * block
        before = before + jnp.sum(jnp.where(t < first_row, oh, 0.0), axis=1, keepdims=True)
        through = through + jnp.sum(jnp.where(t < first_row + rows, oh, 0.0), axis=1, keepdims=True)

    tab_copy.wait()
    lane1 = lax.broadcasted_iota(jnp.int32, (8, 128), 1)
    par = jnp.where(
        lane1 < heads_half, tab[0, 32:40, 0:128], pltpu.roll(tab[1, 32:40, 0:128], heads_half, 1)
    )
    par_t = jnp.transpose(jnp.concatenate([par] * 16, axis=0))[:heads]
    step_f = [par_t[:, v : v + 1] for v in range(4)]
    decay = par_t[:, 4:5] * LOG2E
    skb[...] = jnp.broadcast_to(par_t[:, 5:6], (heads, 128))
    step_r = []
    for v in range(4):
        s = jnp.zeros_like(step_f[0])
        for u in range(4):
            s = s + jnp.where(comp[v] == u, 1.0, 0.0) * step_f[u]
        step_r.append(s)
    log_f = [-decay * s for s in step_f]
    log_r = [-decay * s for s in step_r]

    def mixv(cols, r):
        acc = cols[0] * r[0:1]
        for v in range(1, 4):
            acc = acc + cols[v] * r[v : v + 1]
        return acc

    tlane = lax.broadcasted_iota(jnp.int32, (heads, block), 1)
    centry = lax.broadcasted_iota(jnp.int32, (384, block), 0)
    wf = jnp.zeros((2 * heads, 384), F32)
    wr = jnp.zeros((2 * heads, 384), F32)
    for j in range(n):
        counts, oh = cnt_all[j], oh_all[j]
        t = tlane + j * block
        ef = jnp.where(t < first_row, mixv(log_f, before - counts), 0.0)
        er = jnp.where(t >= first_row + rows, mixv(log_r, counts - oh - through), 0.0)
        pf = jnp.where(t < first_row, jnp.exp2(ef) * mixv(step_f, oh), 0.0)
        pr = jnp.where(t >= first_row + rows, jnp.exp2(er) * mixv(step_r, oh), 0.0)
        hot_f = (centry == taps_f[j, 4:5, :]).astype(BF)
        hot_r = (centry == taps_r[j, 4:5, :]).astype(BF)
        wf = wf + dot(jnp.concatenate(split2(pf), axis=0), hot_f, NT)
        wr = wr + dot(jnp.concatenate(split2(pr), axis=0), hot_r, NT)
    went[0] = wf[:heads] + wf[heads:]
    went[1] = wr[:heads] + wr[heads:]

    local_at = pl.ds(pl.multiple_of(tp * rows, 128), rows)
    counts = cnt_all[me, :, local_at]
    oh = oh_all[me, :, local_at]
    l_f = mixv(log_f, counts - before)
    l_r = mixv(log_r, through - counts + oh)
    lrow[0] = l_f
    lrow[1] = l_r
    lsrc[0] = l_f - jnp.log2(mixv(step_f, oh))
    lsrc[1] = l_r - jnp.log2(mixv(step_r, oh))

    def hot16(taps, width):
        r = lax.broadcasted_iota(jnp.int32, (16, width), 0)
        k, v = r // 4, r % 4
        chosen = jnp.where(k == 0, taps[0], jnp.where(k == 1, taps[1], jnp.where(k == 2, taps[2], taps[3])))
        hot = jnp.where(chosen == v, 1.0, 0.0)
        return jnp.concatenate([hot, hot, hot], axis=0).astype(BF)

    tf = taps_f[me, :, local_at]
    tr = taps_r[me, :, local_at]
    hot_rows = [hot16([x[k : k + 1] for k in range(4)], rows) for x in (tf, tr)]
    codes = lax.broadcasted_iota(jnp.int32, (8, 256), 1)
    edge_f = taps_f[0, :, 0:128]
    edge_r = pltpu.roll(taps_r[n - 1, :, block - 128 :], 8, 1)
    edge = jnp.where(lane1 < 4, edge_f, edge_r)
    table_taps = []
    for k in range(4):
        digit = (codes[0:1] // (4 ** (3 - k))) % 4
        table_taps.append(jnp.concatenate([digit, edge[k : k + 1]], axis=1))
    hot_table = hot16(table_taps, 384)

    def tap_table(conv, proj):
        width = conv.shape[1]
        r = lax.broadcasted_iota(jnp.int32, (16, width), 0)
        k, v = r // 4, r % 4
        c = jnp.where(k == 0, conv[0:1], jnp.where(k == 1, conv[1:2], jnp.where(k == 2, conv[2:3], conv[3:4])))
        p = jnp.where(v == 0, proj[0:1], jnp.where(v == 1, proj[1:2], jnp.where(v == 2, proj[2:3], proj[3:4])))
        return jnp.concatenate(split3(c * p), axis=0)

    ct_state = tap_table(cs_ref[...], sproj[0:4, :])
    btab[...] = silu(dot(ct_state[:, :state], hot_table, TN))
    ri = lax.broadcasted_iota(jnp.int32, (rows, rows), 0)
    ci = lax.broadcasted_iota(jnp.int32, (rows, rows), 1)
    for s in range(2):
        maps = silu(dot(hot_rows[s], ct_state, TN))
        cmat[s] = maps[:, state:]
        seen = (ri >= ci) if s == 0 else (ri <= ci)
        gmat[s] = jnp.where(seen, dot3(maps[:, state:], maps[:, :state], NT), 0.0)

    own_hot = jnp.concatenate([oh[0:8]] * 3 + [jnp.zeros((24, rows), F32)], axis=0).astype(BF)
    rev_oh = jnp.zeros((8, rows), F32)
    sub_r = lax.broadcasted_iota(jnp.int32, (8, rows), 0)
    rev_oh = (tr[3:4] == sub_r).astype(F32)
    rev_hot = jnp.concatenate([rev_oh] * 3 + [jnp.zeros((24, rows), F32)], axis=0).astype(BF)
    for p in range(2):
        for q in range(4):
            width = half // 4
            lo = q * width
            at = slice(p * half + lo, p * half + lo + width)
            ct = tap_table(tab[p, 16:20, lo : lo + width], tab[p, 8:12, lo : lo + width])
            vtab[:, at] = silu(dot(hot_table, ct, TN))
            g8 = silu(tab[p, 0:8, lo : lo + width])
            r8 = lax.broadcasted_iota(jnp.int32, (8, width), 0)
            g8 = jnp.where(r8 < 4, g8, 0.0)
            gh, gm, gl = split3(g8)
            gt = jnp.concatenate(
                [gh.astype(F32), gm.astype(F32), gl.astype(F32), jnp.zeros((24, width), F32)], axis=0
            ).astype(BF)
            for s in range(2):
                xs[s, :, at] = silu(dot(hot_rows[s], ct, TN))
                gate[s, :, at] = dot((own_hot, rev_hot)[s], gt, TN)

    accs[...] = jnp.zeros_like(accs)
    low = lax.broadcasted_iota(jnp.int32, (rows, 128), 1) < 64
    low_c = lax.broadcasted_iota(jnp.int32, (384, 128), 1) < 64

    for s in range(2):
        c_hi, c_lo = split2(cmat[s])
        b_hi, b_lo = split2(btab[...])
        seen = (ri >= ci) if s == 0 else (ri <= ci)

        def pair(q, carry):
            at = pl.ds(pl.multiple_of(q * 128, 128), 128)
            x = xs[s, :, at]
            x_hi, x_lo = split2(x)
            both = jnp.concatenate([x_hi, x_lo], axis=1)
            ys, cols, ws = [], [], []
            for a in range(2):
                h = 2 * q + a
                col = jnp.transpose(rows_of(lrow[s, pl.ds(h, 1), :], 128))
                wide = jnp.concatenate([col] * (rows // 128), axis=1)
                e = jnp.where(seen, wide - lsrc[s, pl.ds(h, 1), :], -1e30)
                d_hi, d_lo = split2(jnp.exp2(e) * gmat[s])
                r = dot(d_hi, both)
                ys.append(r[:, :128] + r[:, 128:] + dot(d_lo, x_hi))
                cols.append(col)
                ws.append(jnp.transpose(rows_of(went[s, pl.ds(h, 1), :], 128)))
            y = jnp.where(low, ys[0], ys[1])
            vw_hi, vw_lo = split2(vtab[:, at] * jnp.where(low_c, ws[0], ws[1]))
            mem = dot(b_hi, vw_hi) + dot(b_lo, vw_hi) + dot(b_hi, vw_lo)
            m_hi, m_lo = split2(mem)
            carried = dot(c_hi, m_hi) + dot(c_lo, m_hi) + dot(c_hi, m_lo)
            y = y + carried * jnp.exp2(jnp.where(low, cols[0], cols[1]))
            sk = jnp.where(low[0:1], skb[pl.ds(2 * q, 1), :], skb[pl.ds(2 * q + 1, 1), :])
            g = (y + sk * x) * gate[s, :, at]
            gated[s, :, at] = g
            accs[s] = accs[s] + g * g
            return carry

        lax.fori_loop(0, pairs, pair, 0)

    scales = [
        lax.rsqrt(jnp.sum(accs[s], axis=1, keepdims=True) / inner + EPSILON) for s in range(2)
    ]
    wo_copy.wait()
    wo_remote.wait()
    out_ref[...] = jnp.zeros_like(out_ref)
    step_k = 256
    for p in range(2):
        def project_out(q, carry):
            lo = pl.multiple_of(q * step_k, step_k)
            at = pl.ds(pl.multiple_of(p * half + q * step_k, step_k), step_k)
            mixed = (gated[0, :, at] * scales[0] + gated[1, :, at] * scales[1]) * tab[
                p, 24:25, pl.ds(lo, step_k)
            ]
            out_ref[...] += dot3(mixed, wout[p, pl.ds(lo, step_k), :])
            return carry

        lax.fori_loop(0, half // step_k, project_out, 0)


def local(
    nucleotides, complement, embedding, w_gate, w_value, w_state, w_step, step_bias,
    decay_rate, conv_value, conv_state, skip_gain, norm_weight, w_out,
):
    n = lax.axis_size("ctx")
    block = nucleotides.shape[0]
    rows = block // 2
    half = w_gate.shape[1]
    depth = w_gate.shape[0]
    inner = 2 * half
    heads = 2 * step_bias.shape[0]
    state = w_state.shape[1] // 2
    vm = pl.BlockSpec(memory_space=pltpu.VMEM)
    hbm = pl.BlockSpec(memory_space=pl.ANY)
    sm = pl.BlockSpec(memory_space=pltpu.SMEM)
    dma = pltpu.SemaphoreType.DMA
    return pl.pallas_call(
        functools.partial(kernel, n),
        out_shape=jax.ShapeDtypeStruct((rows, w_out.shape[1]), F32),
        in_specs=[vm, sm, vm, hbm, hbm, hbm, vm, vm, vm, vm, vm, vm, vm, hbm],
        out_specs=vm,
        scratch_shapes=[
            pltpu.VMEM((n, 1, block), jnp.int32),
            pltpu.VMEM((2, 40, half), F32),
            pltpu.VMEM((2, half, w_out.shape[1]), F32),
            pltpu.VMEM((4, depth, half // 2), F32),
            pltpu.VMEM((depth, 2 * state), F32),
            pltpu.VMEM((4, depth, 128), F32),
            pltpu.VMEM((8, 2 * state), F32),
            pltpu.VMEM((n, 8, block), jnp.int32),
            pltpu.VMEM((n, 8, block), jnp.int32),
            pltpu.VMEM((n, 8, block), F32),
            pltpu.VMEM((n, 8, block), F32),
            pltpu.VMEM((384, inner), F32),
            pltpu.VMEM((2, rows, inner), F32),
            pltpu.VMEM((8, 128), F32),
            pltpu.VMEM((2, rows, inner), F32),
            pltpu.VMEM((2, rows, inner), F32),
            pltpu.VMEM((2, heads, rows), F32),
            pltpu.VMEM((2, heads, rows), F32),
            pltpu.VMEM((2, heads, 384), F32),
            pltpu.VMEM((heads, 128), F32),
            pltpu.VMEM((2, rows, rows), F32),
            pltpu.VMEM((2, rows, state), F32),
            pltpu.VMEM((state, 384), F32),
            pltpu.VMEM((2, rows, 128), F32),
            dma((5,)),
            dma((n - 1,)),
            dma((n - 1,)),
            dma, dma, dma, dma, dma,
        ],
        compiler_params=pltpu.CompilerParams(
            collective_id=0, has_side_effects=True, vmem_limit_bytes=60 * 1024 * 1024
        ),
    )(
        nucleotides[None, :], complement, embedding, w_gate, w_value, w_state, w_step,
        step_bias[None, :], decay_rate[None, :], conv_value, conv_state, skip_gain[None, :],
        norm_weight[None, :], w_out,
    )


def solution(mesh):
    placed = (
        P(("dp", "ctx")), P(), P(), P(None, "tp"), P(None, "tp"), P(), P(None, "tp"),
        P("tp"), P("tp"), P(None, "tp"), P(), P("tp"), P("tp"), P("tp", None),
    )
    return jax.shard_map(
        local, mesh=mesh, in_specs=placed, out_specs=P(("dp", "ctx", "tp"), None), check_vma=False
    )
```

profile of v0, /device:TPU:0, one launch (start us, length us, event | category | flops | bytes accessed | tf_op | source)
XLA Modules:
  0.0 50.1 jit_solution(2388556256616473577)
XLA Ops:
  0.0 1.8 %copy.15.wstep_ref = f32[1024,16]{1,0:T(8,128)} copy(f32[1024,16]{0,1:T(8,128)} %param.20) | data formatting | bytes 131072 | tf_op args[6]
  1.8 45.9 %shard_map.136 = f32[256,1024]{1,0:T(8,128)} custom-call(s32[1,512]{1,0:T(1,128)} %bitcast.6, s32[4]{0:T(128)} %comp_ref.1, f32[4,1024]{1,0:T(4,128)} %emb_ref.1, f32[1024,1024]{1,0:T(8,128)} %wg_ref.1, f32[1024,1024]{1,0:T(8,128)} %wv_ref.1, f32[1024,256]{1,0:T(8,128)} %ws_ref.1, f32[1024,16]{1,0:T(8,128)} %copy.15.wstep_ref, f32[1,16]{1,0:T(1,128)} %bitcast.7, ...), custom_call_target="tpu_custom_call" | custom-call | tf_op jit(solution)/shard_map/pallas_call | solution.py:391
  47.8 2.3 %copy.17 = f32[256,1024]{1,0:T(8,128)} copy(f32[256,1024]{1,0:T(8,128)} %shard_map.136) | data formatting | bytes 2097152
where the time goes:
time: 50.3 us; the launch traced here: 50.1 us
  Pallas kernels  45.9 us (91%)
  local copies, waits for them, and re-layouts  4.14 us (8%)
    pallas_call x1, Pallas kernels, local(): pl.pallas_call(functools.partial(kernel, n), out_shape=jax.ShapeDtypeStru...  45.9 us
    unnamed x2, local copies, waits for them, and re-layouts  4.14 us

commit v1 on v0

--- a/solution.py
+++ b/solution.py
@@ -40,7 +40,8 @@
 
 
 def silu(x):
-    return x / (1.0 + jnp.exp(-x))
+    half = 0.5 * x
+    return half + half * jnp.tanh(half)
 
 
 def rows_of(x, count):
@@ -51,7 +52,7 @@
     n, ids_ref, comp_ref, emb_ref, wg_ref, wv_ref, ws_ref, wstep_ref, bias_ref, decay_ref,
     cv_ref, cs_ref, skip_ref, nw_ref, wo_ref, out_ref,
     ids_all, tab, wout, wbuf, wsbuf, ebc, sproj, taps_f, taps_r, cnt_all, oh_all,
-    vtab, xs, xp, gate, gated, lrow, lsrc, went, skb, gmat, cmat, btab, accs,
+    vtab, xs, xp, gate, gated, lrow, lsrc, went, skb, gmat, cmat, btab, accs, ccat, bcat, becat,
     loc_sem, id_send, id_recv, tab_send, tab_recv, wo_send, wo_recv, wo_loc,
 ):
     me = lax.axis_index("ctx")
@@ -133,11 +134,13 @@
             tab[tp, pl.ds(base + v, 1), pl.ds((i % 2) * chunk, chunk)] = parts[v]
     tab[tp, 16:20, :] = cv_ref[...]
     tab[tp, 24:25, :] = nw_ref[...]
-    raw = project(wstep_ref, heads_half)
     for v in range(4):
-        z = raw[v] + bias_ref[...]
-        step = jnp.maximum(z, 0.0) + jnp.log1p(jnp.exp(-jnp.abs(z)))
-        tab[tp, 32 + v : 33 + v, 0:heads_half] = step
+        z = jnp.sum(wstep_ref[...] * emb_ref[v : v + 1, :], axis=1, keepdims=True)
+        xp[:, v : v + 1] = z
+    raw = jnp.transpose(jnp.concatenate([xp[...]] * (128 // heads_half), axis=0))
+    z = raw[0:8, 0:heads_half] + bias_ref[...]
+    step = jnp.maximum(z, 0.0) + jnp.log1p(jnp.exp(-jnp.abs(z)))
+    tab[tp, 32:36, 0:heads_half] = step[0:4]
     tab[tp, 36:37, 0:heads_half] = decay_ref[...]
     tab[tp, 37:38, 0:heads_half] = skip_ref[...]
     tab_copy = pltpu.make_async_remote_copy(
@@ -301,7 +304,8 @@
             lo = q * width
             at = slice(p * half + lo, p * half + lo + width)
             ct = tap_table(tab[p, 16:20, lo : lo + width], tab[p, 8:12, lo : lo + width])
-            vtab[:, at] = silu(dot(hot_table, ct, TN))
+            vtab[0:256, at] = silu(dot(hot_table[:, :256], ct, TN))
+            vtab[256:272, at] = silu(dot(hot_table[:, 256:], ct, TN)[:16])
             g8 = silu(tab[p, 0:8, lo : lo + width])
             r8 = lax.broadcasted_iota(jnp.int32, (8, width), 0)
             g8 = jnp.where(r8 < 4, g8, 0.0)
@@ -314,43 +318,82 @@
                 gate[s, :, at] = dot((own_hot, rev_hot)[s], gt, TN)
 
     accs[...] = jnp.zeros_like(accs)
+    mid = rows // 2
     low = lax.broadcasted_iota(jnp.int32, (rows, 128), 1) < 64
-    low_c = lax.broadcasted_iota(jnp.int32, (384, 128), 1) < 64
-
+    tri_r = lax.broadcasted_iota(jnp.int32, (mid, mid), 0)
+    tri_c = lax.broadcasted_iota(jnp.int32, (mid, mid), 1)
     for s in range(2):
-        c_hi, c_lo = split2(cmat[s])
-        b_hi, b_lo = split2(btab[...])
-        seen = (ri >= ci) if s == 0 else (ri <= ci)
-
-        def pair(q, carry):
-            at = pl.ds(pl.multiple_of(q * 128, 128), 128)
+        ccat[s] = jnp.concatenate(split2(cmat[s]), axis=1)
+    b_hi, b_lo = split2(btab[...])
+    bcat[...] = jnp.concatenate([b_hi[:, :256], b_lo[:, :256]], axis=0)
+    e_hi = b_hi[:, 256:].astype(F32)
+    e_lo = pltpu.roll(b_lo[:, 256:].astype(F32), 16, 1)
+    elane = lax.broadcasted_iota(jnp.int32, (state, 128), 1)
+    becat[...] = jnp.where(elane < 16, e_hi, jnp.where(elane < 32, e_lo, 0.0)).astype(BF)
+
+    def heads_rows(ref, s, h, at):
+        return jnp.concatenate(
+            [rows_of(ref[s, pl.ds(h, 1), :][:, at], 64), rows_of(ref[s, pl.ds(h + 1, 1), :][:, at], 64)], axis=0
+        )
+
+    def pair(q, carry):
+        at = pl.ds(pl.multiple_of(q * 128, 128), 128)
+        vt, ve = vtab[0:256, at], vtab[256:272, at]
+        sk = jnp.where(low[0:1], skb[pl.ds(2 * q, 1), :], skb[pl.ds(2 * q + 1, 1), :])
+        for s in range(2):
+            near = slice(0, mid) if s == 0 else slice(mid, rows)
+            far = slice(mid, rows) if s == 0 else slice(0, mid)
+            seen = (tri_r >= tri_c) if s == 0 else (tri_r <= tri_c)
             x = xs[s, :, at]
             x_hi, x_lo = split2(x)
             both = jnp.concatenate([x_hi, x_lo], axis=1)
-            ys, cols, ws = [], [], []
+            near_both = jnp.concatenate([both[near], both[near]], axis=0)
+            near_l, far_hi, far_lo, cols = [], [], [], []
             for a in range(2):
                 h = 2 * q + a
                 col = jnp.transpose(rows_of(lrow[s, pl.ds(h, 1), :], 128))
-                wide = jnp.concatenate([col] * (rows // 128), axis=1)
-                e = jnp.where(seen, wide - lsrc[s, pl.ds(h, 1), :], -1e30)
-                d_hi, d_lo = split2(jnp.exp2(e) * gmat[s])
-                r = dot(d_hi, both)
-                ys.append(r[:, :128] + r[:, 128:] + dot(d_lo, x_hi))
+                src = lsrc[s, pl.ds(h, 1), :]
+                def decayed(i, j, masked):
+                    e = col[i] - src[:, j]
+                    if masked:
+                        e = jnp.where(seen, e, -1e30)
+                    return split2(jnp.exp2(e) * gmat[s, i, j])
+                nn_hi, nn_lo = decayed(near, near, True)
+                ff_hi, ff_lo = decayed(far, far, True)
+                fn_hi, fn_lo = decayed(far, near, False)
+                near_l.append(jnp.concatenate([nn_hi, nn_lo], axis=1))
+                order = (fn_hi, ff_hi) if s == 0 else (ff_hi, fn_hi)
+                far_hi.append(jnp.concatenate(order, axis=1))
+                order = (fn_lo, ff_lo) if s == 0 else (ff_lo, fn_lo)
+                far_lo.append(jnp.concatenate(order, axis=1))
                 cols.append(col)
-                ws.append(jnp.transpose(rows_of(went[s, pl.ds(h, 1), :], 128)))
-            y = jnp.where(low, ys[0], ys[1])
-            vw_hi, vw_lo = split2(vtab[:, at] * jnp.where(low_c, ws[0], ws[1]))
-            mem = dot(b_hi, vw_hi) + dot(b_lo, vw_hi) + dot(b_hi, vw_lo)
-            m_hi, m_lo = split2(mem)
-            carried = dot(c_hi, m_hi) + dot(c_lo, m_hi) + dot(c_hi, m_lo)
+            rn = dot(jnp.concatenate(near_l, axis=0), near_both)
+            rf = dot(jnp.concatenate(far_hi, axis=0), both)
+            rl = dot(jnp.concatenate(far_lo, axis=0), x_hi)
+            rn = rn[:, :128] + rn[:, 128:]
+            rf = rf[:, :128] + rf[:, 128:] + rl
+            lowm = low[:mid]
+            yn = jnp.where(lowm, rn[:mid], rn[mid:])
+            yf = jnp.where(lowm, rf[:mid], rf[mid:])
+            y = jnp.concatenate([yn, yf] if s == 0 else [yf, yn], axis=0)
+            w = jnp.transpose(heads_rows(went, s, 2 * q, slice(0, 256)))
+            we = jnp.transpose(heads_rows(went, s, 2 * q, slice(256, 384)))[:16]
+            vw = jnp.concatenate(split2(vt * w), axis=1)
+            vwe = jnp.concatenate(split2(ve * we), axis=1)
+            vwe = jnp.concatenate([vwe, vwe], axis=0)
+            r = dot(bcat[...], vw)
+            r = r[:state] + r[state:] + dot(becat[:, 0:32], vwe)
+            mem = r[:, :128] + r[:, 128:]
+            m2 = jnp.concatenate(split2(mem), axis=1)
+            carried = dot(ccat[s], jnp.concatenate([m2, m2], axis=0))
+            carried = carried[:, :128] + carried[:, 128:]
             y = y + carried * jnp.exp2(jnp.where(low, cols[0], cols[1]))
-            sk = jnp.where(low[0:1], skb[pl.ds(2 * q, 1), :], skb[pl.ds(2 * q + 1, 1), :])
             g = (y + sk * x) * gate[s, :, at]
             gated[s, :, at] = g
             accs[s] = accs[s] + g * g
-            return carry
-
-        lax.fori_loop(0, pairs, pair, 0)
+        return carry
+
+    lax.fori_loop(0, pairs, pair, 0)
 
     scales = [
         lax.rsqrt(jnp.sum(accs[s], axis=1, keepdims=True) / inner + EPSILON) for s in range(2)
@@ -405,9 +448,9 @@
             pltpu.VMEM((n, 8, block), jnp.int32),
             pltpu.VMEM((n, 8, block), F32),
             pltpu.VMEM((n, 8, block), F32),
-            pltpu.VMEM((384, inner), F32),
+            pltpu.VMEM((272, inner), F32),
             pltpu.VMEM((2, rows, inner), F32),
-            pltpu.VMEM((8, 128), F32),
+            pltpu.VMEM((heads // 2, 128), F32),
             pltpu.VMEM((2, rows, inner), F32),
             pltpu.VMEM((2, rows, inner), F32),
             pltpu.VMEM((2, heads, rows), F32),
@@ -418,6 +461,9 @@
             pltpu.VMEM((2, rows, state), F32),
             pltpu.VMEM((state, 384), F32),
             pltpu.VMEM((2, rows, 128), F32),
+            pltpu.VMEM((2, rows, 2 * state), BF),
+            pltpu.VMEM((2 * state, 256), BF),
+            pltpu.VMEM((state, 128), BF),
             dma((5,)),
             dma((n - 1,)),
             dma((n - 1,)),
@@ -427,7 +473,7 @@
             collective_id=0, has_side_effects=True, vmem_limit_bytes=60 * 1024 * 1024
         ),
     )(
-        nucleotides[None, :], complement, embedding, w_gate, w_value, w_state, w_step,
+        nucleotides[None, :], complement, embedding, w_gate, w_value, w_state, w_step.T,
         step_bias[None, :], decay_rate[None, :], conv_value, conv_state, skip_gain[None, :],
         norm_weight[None, :], w_out,
     )

time: 50.3 us -> 40.5 us (0.81)
  Pallas kernels: 45.9 us -> 37.9 us
  local copies, waits for them, and re-layouts: 4.14 us -> 2.31 us
    pallas_call x1, Pallas kernels: 45.9 us -> 37.9 us  [local(): pl.pallas_call(functools.partial(kernel, n), out_shape=jax.ShapeDtypeStru...]
    unnamed x2 -> x1, local copies, waits for them, and re-layouts: 4.14 us -> 2.31 us
where the time goes in v1:
time: 40.5 us; the launch traced here: 40.3 us
  Pallas kernels  37.9 us (94%)
  local copies, waits for them, and re-layouts  2.31 us (6%)
    pallas_call x1, Pallas kernels, local(): pl.pallas_call(functools.partial(kernel, n), out_shape=jax.ShapeDtypeStru...  37.9 us
    unnamed x1, local copies, waits for them, and re-layouts  2.31 us

profile of v1, /device:TPU:0, one launch (start us, length us, event | category | flops | bytes accessed | tf_op | source)
XLA Modules:
  0.0 40.3 jit_solution(7179610540407336695)
XLA Ops:
  0.0 37.9 %shard_map.136 = f32[256,1024]{1,0:T(8,128)} custom-call(s32[1,512]{1,0:T(1,128)} %bitcast.8, s32[4]{0:T(128)} %comp_ref.1, f32[4,1024]{1,0:T(4,128)} %emb_ref.1, f32[1024,1024]{1,0:T(8,128)} %wg_ref.1, f32[1024,1024]{1,0:T(8,128)} %wv_ref.1, f32[1024,256]{1,0:T(8,128)} %ws_ref.1, f32[16,1024]{1,0:T(8,128)} %bitcast.6, f32[1,16]{1,0:T(1,128)} %bitcast.9, ...), custom_call_target="tpu_custom_call" | custom-call | tf_op jit(solution)/shard_map/pallas_call | solution.py:434
  37.9 2.3 %copy.16 = f32[256,1024]{1,0:T(8,128)} copy(f32[256,1024]{1,0:T(8,128)} %shard_map.136) | data formatting | bytes 2097152

commit v2 on v1

--- a/solution.py
+++ b/solution.py
@@ -393,7 +393,7 @@
             accs[s] = accs[s] + g * g
         return carry
 
-    lax.fori_loop(0, pairs, pair, 0)
+    lax.fori_loop(0, pairs, pair, 0, unroll=2)
 
     scales = [
         lax.rsqrt(jnp.sum(accs[s], axis=1, keepdims=True) / inner + EPSILON) for s in range(2)

time: 40.5 us -> 38.8 us (0.958)
  Pallas kernels: 37.9 us -> 36.3 us
    pallas_call x1, Pallas kernels: 37.9 us -> 36.3 us  [local(): pl.pallas_call(functools.partial(kernel, n), out_shape=jax.ShapeDtypeStru...]
where the time goes in v2:
time: 38.8 us; the launch traced here: 38.6 us
  Pallas kernels  36.3 us (94%)
  local copies, waits for them, and re-layouts  2.31 us (6%)
    pallas_call x1, Pallas kernels, local(): pl.pallas_call(functools.partial(kernel, n), out_shape=jax.ShapeDtypeStru...  36.3 us
    unnamed x1, local copies, waits for them, and re-layouts  2.31 us

profile of v2, /device:TPU:0, one launch (start us, length us, event | category | flops | bytes accessed | tf_op | source)
XLA Modules:
  0.0 38.6 jit_solution(5570081271166949879)
XLA Ops:
  0.0 36.3 %shard_map.136 = f32[256,1024]{1,0:T(8,128)} custom-call(s32[1,512]{1,0:T(1,128)} %bitcast.8, s32[4]{0:T(128)} %comp_ref.1, f32[4,1024]{1,0:T(4,128)} %emb_ref.1, f32[1024,1024]{1,0:T(8,128)} %wg_ref.1, f32[1024,1024]{1,0:T(8,128)} %wv_ref.1, f32[1024,256]{1,0:T(8,128)} %ws_ref.1, f32[16,1024]{1,0:T(8,128)} %bitcast.6, f32[1,16]{1,0:T(1,128)} %bitcast.9, ...), custom_call_target="tpu_custom_call" | custom-call | tf_op jit(solution)/shard_map/pallas_call | solution.py:434
  36.3 2.3 %copy.16 = f32[256,1024]{1,0:T(8,128)} copy(f32[256,1024]{1,0:T(8,128)} %shard_map.136) | data formatting | bytes 2097152
